TPU v7x, 32 devices: a whole 2x2x4 slice. The times are simulated.
32 devices in a mesh: dom: 8 (over z, y), feat: 4 (over x, core).
Axes of the slice: x: 2, y: 2, z: 4, core: 2. Of those that a mesh axis runs over, the one named last changes fastest.
Arguments:
- features: bfloat16 [32768, 512], P('dom', 'feat'), may hold values from -6 to 6
- theta: bfloat16 [512, 512], P(None, 'feat'), may hold values from -0.25 to 0.25
- incidence: int32 [3, 4096], P(None, 'dom'), may hold values from 0 to 4095, as said below
- edge_weight: float32 [16384], P('dom'), may hold values from 0.5 to 2
- cotangent: bfloat16 [32768, 512], P('dom', 'feat'), may hold values from -6 to 6
Outputs:
- activation: bfloat16 [32768, 512], P('dom', 'feat')
- grad_features: bfloat16 [32768, 512], P('dom', 'feat')
- grad_theta: float32 [512, 512], P('dom', 'feat')
Inputs may be any that keep to these rules, and one draw needn't show every extreme that they name: `incidence`: in the 64 slots from one vertex owner to one hyperedge owner the live slots (weight over zero) come first, at least one of them; some hyperedge owner receives all 64 slots live from every vertex owner.
All inputs are finite; a program needn't handle non-finite values.
Results may differ from a plain program's by a relative error of at most 0.0073.
Values may be sent and summed in bfloat16 or wider, within the bound.
A program may use at most 64 MiB of HBM per device.

v0:
```python
import jax
import jax.numpy as jnp
from jax import lax
from jax.sharding import PartitionSpec as P


def local(features, theta, incidence, edge_weight, cotangent):
    owners = lax.axis_size("dom")
    nvert = features.shape[0]
    cols = features.shape[1]
    nedge = edge_weight.shape[0]
    vert = incidence[0]
    edge = incidence[1]
    weight = incidence[2]
    weight_f = weight.astype(jnp.float32)
    dvis = lax.rsqrt(1.0 + jax.ops.segment_sum(weight_f, vert, num_segments=nvert))
    slot_scale = weight_f * dvis[vert]
    full_rows = lax.all_gather(features, "feat", axis=1, tiled=True)
    projected = jnp.dot(full_rows, theta, preferred_element_type=jnp.float32).astype(jnp.bfloat16)
    message = (slot_scale[:, None] * projected[vert].astype(jnp.float32)).astype(jnp.bfloat16)
    recv_rows, recv_edge, recv_weight = (
        lax.all_to_all(
            message.reshape(owners, -1, cols), "dom", split_axis=0, concat_axis=0, tiled=True
        ),
        lax.all_to_all(edge.reshape(owners, -1), "dom", split_axis=0, concat_axis=0, tiled=True),
        lax.all_to_all(weight.reshape(owners, -1), "dom", split_axis=0, concat_axis=0, tiled=True),
    )
    recv_edge = recv_edge.reshape(-1)
    degree = 1.0 + jax.ops.segment_sum(
        recv_weight.reshape(-1).astype(jnp.float32), recv_edge, num_segments=nedge
    )
    edge_scale = edge_weight / degree

    def edge_side(rows):
        edge_sum = jax.ops.segment_sum(
            rows.reshape(-1, cols).astype(jnp.float32), recv_edge, num_segments=nedge
        )
        edge_rows = (edge_scale[:, None] * edge_sum).astype(jnp.bfloat16)
        return edge_rows[recv_edge].reshape(owners, -1, cols)

    def vertex_side(back):
        terms = weight_f[:, None] * back.reshape(-1, cols).astype(jnp.float32)
        return dvis[:, None] * jax.ops.segment_sum(terms, vert, num_segments=nvert)

    back = lax.all_to_all(edge_side(recv_rows), "dom", split_axis=0, concat_axis=0, tiled=True)
    summed = vertex_side(back)
    sigma = jax.nn.sigmoid(summed)
    activation = (summed * sigma).astype(jnp.bfloat16)
    slope = sigma * (1.0 + summed * (1.0 - sigma))
    grad_summed = cotangent.astype(jnp.float32) * slope
    grad_message = (slot_scale[:, None] * grad_summed[vert]).astype(jnp.bfloat16)
    grad_recv = lax.all_to_all(
        grad_message.reshape(owners, -1, cols), "dom", split_axis=0, concat_axis=0, tiled=True
    )
    grad_back = lax.all_to_all(edge_side(grad_recv), "dom", split_axis=0, concat_axis=0, tiled=True)
    grad_projected = vertex_side(grad_back).astype(jnp.bfloat16)
    theta_full = lax.all_gather(theta, "feat", axis=1, tiled=True)
    theta_mine = lax.dynamic_slice_in_dim(theta_full, lax.axis_index("feat") * cols, cols, 0)
    grad_total = lax.dot_general(
        lax.all_gather(grad_projected, "feat", axis=1, tiled=True),
        theta_mine,
        (((1,), (1,)), ((), ())),
        preferred_element_type=jnp.float32,
    )
    grad_features = grad_total.astype(jnp.bfloat16)
    share = full_rows.shape[1] // owners
    term = lax.dot_general(
        full_rows, grad_projected, (((0,), (0,)), ((), ())), preferred_element_type=jnp.float32
    )
    total = lax.psum(term, "dom")
    grad_theta = lax.dynamic_slice_in_dim(total, lax.axis_index("dom") * share, share, 0)
    return (activation, grad_features, grad_theta)


def solution(mesh):
    placed = (P("dom", "feat"), P(None, "feat"), P(None, "dom"), P("dom"), P("dom", "feat"))
    return jax.shard_map(
        local,
        mesh=mesh,
        in_specs=placed,
        out_specs=(P("dom", "feat"), P("dom", "feat"), P("dom", "feat")),
        check_vma=False,
    )
```

profile of v0, /device:TPU:0, one launch (start us, length us, event | category | flops | bytes accessed | tf_op | source)
XLA Modules:
  0.0 234.5 jit_solution(12169646869658793668)
XLA Ops:
  7.9 0.8 slice_reduce_fusion.1
  9.4 7.3 %all-to-all-start = ((s32[8,1,64]{2,1,0:T(1,128)}), s32[8,1,64]{2,1,0:T(1,128)S(1)}, u32[]{:S(2)}, u32[]{:S(2)}) async-start(s32[8,1,64]{2,1,0:T(1,128)} %all_to_all.24), calls=%async_computation | async-start | bytes 8192 | tf_op jit(solution)/shard_map/all_to_all | solution.py:25
  17.4 0.7 fusion.19
  18.8 4.3 %all-to-all-done = s32[8,1,64]{2,1,0:T(1,128)S(1)} async-done(((s32[8,1,64]{2,1,0:T(1,128)}), s32[8,1,64]{2,1,0:T(1,128)S(1)}, u32[]{:S(2)}, u32[]{:S(2)}) %all-to-all-start) | async-done | bytes 2080 | tf_op jit(solution)/shard_map/all_to_all | solution.py:25
  23.1 3.3 %all-to-all-start.1 = ((s32[8,1,64]{2,1,0:T(1,128)}), s32[8,1,64]{2,1,0:T(1,128)S(1)}, u32[]{:S(2)}, u32[]{:S(2)}) async-start(s32[8,1,64]{2,1,0:T(1,128)} %all_to_all.26), calls=%async_computation.1 | async-start | bytes 8192 | tf_op jit(solution)/shard_map/all_to_all | solution.py:26
  26.5 3.3 %scatter_custom_fusion = f32[4096]{0:T(1024)S(1)} fusion(s32[512]{0:T(512)S(1)} %bitcast.41, f32[512]{0:T(512)S(1)} %bitcast.36, f32[]{:T(128)} %constant.11.clone.1), kind=kCustom, calls=%fused_computation.40 | custom fusion | flops 512 | bytes 16388 | tf_op jit(solution)/shard_map/scatter-add | solution.py:16
  29.8 3.1 %gather_fusion = f32[512]{0:T(512)S(1)} fusion(f32[4096]{0:T(1024)S(1)} %rsqrt.3, s32[1024]{0:T(1024)S(1)} %pad_clamp_fusion.1), kind=kCustom, calls=%fused_computation | custom fusion | bytes 6144 | tf_op jit(solution)/shard_map/gather | solution.py:17
  34.4 3.3 %scatter_custom_fusion.1 = f32[2048]{0:T(1024)S(1)} fusion(s32[512]{0:T(512)S(1)} %reshape.181, f32[512]{0:T(512)S(1)} %reshape.183, f32[]{:T(128)} %constant.11.clone.1), kind=kCustom, calls=%fused_computation.45 | custom fusion | flops 512 | bytes 8196 | tf_op jit(solution)/shard_map/scatter-add | solution.py:29
  37.7 9.6 %all-gather.3.cloned.1.call-done = bf16[4096,512]{1,0:T(8,128)(2,1)} async-done(((bf16[4096,128]{1,0:T(8,128)(2,1)}), bf16[4096,512]{1,0:T(8,128)(2,1)}) %all-gather.3.cloned.1.call-update) | async-done | bytes 4194320 | tf_op jit(solution)/shard_map/all_gather | solution.py:18
  47.3 3.4 %convolution_convert_fusion.1 = bf16[4096,128]{1,0:T(8,128)(2,1)S(1)} fusion(bf16[4096,512]{1,0:T(8,128)(2,1)} %all-gather.3.cloned.1.call-done, bf16[512,128]{1,0:T(8,128)(2,1)S(1)} %copy-done.2), kind=kOutput, calls=%fused_computation.12 | convolution fusion | flops 537395200 | bytes 5373952 | tf_op jit(solution)/shard_map/dot_general | solution.py:19
  50.8 1.3 gather_fusion.1
  52.1 0.8 fusion.10
  52.9 5.5 %all-to-all-start.2 = ((bf16[8,64,128]{2,1,0:T(8,128)(2,1)}), bf16[8,64,128]{2,1,0:T(8,128)(2,1)S(1)}, u32[]{:S(2)}, u32[]{:S(2)}) async-start(bf16[8,64,128]{2,1,0:T(8,128)(2,1)} %fusion.10), calls=%async_computation.2 | async-start | bytes 262144 | tf_op jit(solution)/shard_map/all_to_all | solution.py:22
  58.5 7.3 %all-to-all-done.2 = bf16[8,64,128]{2,1,0:T(8,128)(2,1)S(1)} async-done(((bf16[8,64,128]{2,1,0:T(8,128)(2,1)}), bf16[8,64,128]{2,1,0:T(8,128)(2,1)S(1)}, u32[]{:S(2)}, u32[]{:S(2)}) %all-to-all-start.2) | async-done | bytes 131104 | tf_op jit(solution)/shard_map/all_to_all | solution.py:22
  65.8 2.5 %scatter_custom_fusion.2 = f32[2048,128]{1,0:T(8,128)S(1)} fusion(s32[512]{0:T(512)S(1)} %reshape.181, f32[]{:T(128)} %constant.12.clone.1, bf16[512,128]{1,0:T(8,128)(2,1)S(1)} %bitcast.28), kind=kCustom, calls=%fused_computation.26 | custom fusion | flops 131072 | bytes 1179652 | tf_op jit(solution)/shard_map/scatter-add | solution.py:35
  68.7 1.3 gather_fusion.2
  70.1 9.9 %all_to_all.38 = bf16[8,64,128]{2,1,0:T(8,128)(2,1)S(1)} all-to-all(bf16[8,64,128]{2,1,0:T(8,128)(2,1)S(1)} %bitcast.33), channel_id=1, replica_groups=mesh['dom'=8,'feat'=4] {'dom'}, dimensions={0} | all-to-all | bytes 262144 | tf_op jit(solution)/shard_map/all_to_all | solution.py:45
  79.9 3.8 %scatter_custom_fusion.3 = f32[4096,128]{1,0:T(8,128)} fusion(s32[512]{0:T(512)S(1)} %bitcast.42, f32[]{:T(128)} %constant.12.clone.1, bf16[512,128]{1,0:T(8,128)(2,1)S(1)} %bitcast.34, f32[512]{0:T(512)S(1)} %bitcast.37), kind=kCustom, calls=%fused_computation.22 | custom fusion | flops 196608 | bytes 2230276 | tf_op jit(solution)/shard_map/scatter-add | solution.py:43
  83.7 3.2 %multiply_multiply_fusion = (f32[4096,128]{1,0:T(8,128)S(1)}, bf16[4096,128]{1,0:T(8,128)(2,1)}) fusion(bf16[4096,128]{1,0:T(8,128)(2,1)S(1)} %copy-done.1, f32[4096,128]{1,0:T(8,128)} %scatter_custom_fusion.3, f32[4096]{0:T(1024)S(1)} %rsqrt.3), kind=kLoop, calls=%fused_computation.14 | loop fusion | flops 6291456 | bytes 6307840 | tf_op jit(solution)/shard_map/mul | solution.py:50
  86.9 1.0 gather_fusion.3
  88.1 9.7 %all_to_all.39 = bf16[8,64,128]{2,1,0:T(8,128)(2,1)S(1)} all-to-all(bf16[8,64,128]{2,1,0:T(8,128)(2,1)S(1)} %multiply_convert_fusion.4), channel_id=1, replica_groups=mesh['dom'=8,'feat'=4] {'dom'}, dimensions={0} | all-to-all | bytes 262144 | tf_op jit(solution)/shard_map/all_to_all | solution.py:52
  97.8 2.5 %scatter_custom_fusion.4 = f32[2048,128]{1,0:T(8,128)S(1)} fusion(s32[512]{0:T(512)S(1)} %reshape.181, f32[]{:T(128)} %constant.12.clone.1, bf16[512,128]{1,0:T(8,128)(2,1)S(1)} %bitcast.30), kind=kCustom, calls=%fused_computation.24 | custom fusion | flops 131072 | bytes 1179652 | tf_op jit(solution)/shard_map/scatter-add | solution.py:35
  100.7 1.3 gather_fusion.4
  102.0 9.7 %all_to_all.40 = bf16[8,64,128]{2,1,0:T(8,128)(2,1)S(1)} all-to-all(bf16[8,64,128]{2,1,0:T(8,128)(2,1)S(1)} %bitcast.31), channel_id=1, replica_groups=mesh['dom'=8,'feat'=4] {'dom'}, dimensions={0} | all-to-all | bytes 262144 | tf_op jit(solution)/shard_map/all_to_all | solution.py:55
  111.7 2.9 %scatter_custom_fusion.5 = f32[4096,128]{1,0:T(8,128)S(1)} fusion(s32[512]{0:T(512)S(1)} %bitcast.43, f32[]{:T(128)} %constant.12.clone.1, bf16[512,128]{1,0:T(8,128)(2,1)S(1)} %bitcast.29, f32[512]{0:T(512)S(1)} %bitcast.38), kind=kCustom, calls=%fused_computation.20 | custom fusion | flops 196608 | bytes 2230276 | tf_op jit(solution)/shard_map/scatter-add | solution.py:43
  114.6 0.7 multiply_convert_fusion
  115.4 4.0 %convolution_bitcast_fusion = f32[512,128]{0,1:T(8,128)} fusion(bf16[4096,128]{1,0:T(8,128)(2,1)S(1)} %multiply_convert_fusion, bf16[4096,512]{1,0:T(8,128)(2,1)} %all-gather.3.cloned.1.call-done), kind=kOutput, calls=%fused_computation.17 | convolution fusion | flops 536870912 | bytes 5505024 | tf_op jit(solution)/shard_map/dot_general | solution.py:67
  120.2 6.5 %all_gather.11 = bf16[512,512]{1,0:T(8,128)(2,1)S(1)} all-gather(bf16[512,128]{1,0:T(8,128)(2,1)S(1)} %copy-done.2), channel_id=1, replica_groups=mesh['dom'=8,'feat'=4] {'feat'}, dimensions={1}, use_global_device_ids=true | all-gather | bytes 655360 | tf_op jit(solution)/shard_map/all_gather | solution.py:57
  126.7 60.3 %all-reduce.2.cloned.1.call-done = f32[512,128]{0,1:T(8,128)} async-done(((f32[512,128]{0,1:T(8,128)}), f32[512,128]{0,1:T(8,128)}) %all-reduce.2.cloned.1.call-update) | async-done | bytes 262160 | tf_op jit(solution)/shard_map/psum | solution.py:70
  187.0 0.9 constant_dynamic-slice_fusion
  188.6 34.9 %all-gather.5.cloned.1.call-done = bf16[4096,512]{1,0:T(8,128)(2,1)} async-done(((bf16[4096,128]{1,0:T(8,128)(2,1)}), bf16[4096,512]{1,0:T(8,128)(2,1)}) %all-gather.5.cloned.1.call-update) | async-done | bytes 4194320 | tf_op jit(solution)/shard_map/all_gather | solution.py:60
  223.5 4.4 %convolution_convert_fusion = bf16[4096,128]{1,0:T(8,128)(2,1)} fusion(bf16[4096,512]{1,0:T(8,128)(2,1)} %all-gather.5.cloned.1.call-done, bf16[512,512]{1,0:T(8,128)(2,1)S(1)} %all_gather.11, s32[]{:T(128)S(6)} %select_n.31), kind=kOutput, calls=%fused_computation.11 | convolution fusion | flops 537395200 | bytes 5373956 | tf_op jit(solution)/shard_map/dot_general | solution.py:59
  (36 shorter events, 6.7 us)
Async XLA Ops:
  7.2 30.6 %copy-start.3 = (f32[2048]{0:T(1024)S(1)}, f32[2048]{0:T(1024)}, u32[]{:S(2)}) copy-start(f32[2048]{0:T(1024)} %param.8) | copy-start | bytes 24580
  7.2 40.2 %copy-start.2 = (bf16[512,128]{1,0:T(8,128)(2,1)S(1)}, bf16[512,128]{1,0:T(8,128)(2,1)}, u32[]{:S(2)}) copy-start(bf16[512,128]{1,0:T(8,128)(2,1)} %param.6) | copy-start | bytes 393220
  7.2 40.1 %all-gather.3.cloned.1.call-start = ((), (), s32[]{:S(2)}) async-start(), calls=%async_computation.6 | async-start | bytes 5242880 | tf_op jit(solution)/shard_map/all_gather | solution.py:18
  9.4 13.7 %all-to-all-start = ((s32[8,1,64]{2,1,0:T(1,128)}), s32[8,1,64]{2,1,0:T(1,128)S(1)}, u32[]{:S(2)}, u32[]{:S(2)}) async-start(s32[8,1,64]{2,1,0:T(1,128)} %all_to_all.24), calls=%async_computation | async-start | bytes 8192 | tf_op jit(solution)/shard_map/all_to_all | solution.py:25
  23.1 11.3 %all-to-all-start.1 = ((s32[8,1,64]{2,1,0:T(1,128)}), s32[8,1,64]{2,1,0:T(1,128)S(1)}, u32[]{:S(2)}, u32[]{:S(2)}) async-start(s32[8,1,64]{2,1,0:T(1,128)} %all_to_all.26), calls=%async_computation.1 | async-start | bytes 8192 | tf_op jit(solution)/shard_map/all_to_all | solution.py:26
  52.9 12.9 %all-to-all-start.2 = ((bf16[8,64,128]{2,1,0:T(8,128)(2,1)}), bf16[8,64,128]{2,1,0:T(8,128)(2,1)S(1)}, u32[]{:S(2)}, u32[]{:S(2)}) async-start(bf16[8,64,128]{2,1,0:T(8,128)(2,1)} %fusion.10), calls=%async_computation.2 | async-start | bytes 262144 | tf_op jit(solution)/shard_map/all_to_all | solution.py:22
  58.4 128.5 %all-reduce.2.cloned.1.call-start = ((), (), s32[]{:S(2)}) async-start(), calls=%async_computation.8 | async-start | bytes 524288 | tf_op jit(solution)/shard_map/psum | solution.py:70
  68.7 15.0 %copy-start.1 = (bf16[4096,128]{1,0:T(8,128)(2,1)S(1)}, bf16[4096,128]{1,0:T(8,128)(2,1)}, u32[]{:S(2)}) copy-start(bf16[4096,128]{1,0:T(8,128)(2,1)} %param.9) | copy-start | bytes 3145732
  115.4 4.1 %copy-start = (bf16[4096,128]{1,0:T(8,128)(2,1)}, bf16[4096,128]{1,0:T(8,128)(2,1)S(1)}, u32[]{:S(2)}) copy-start(bf16[4096,128]{1,0:T(8,128)(2,1)S(1)} %multiply_convert_fusion) | copy-start | bytes 3145732
  119.4 104.1 %all-gather.5.cloned.1.call-start = ((), (), s32[]{:S(2)}) async-start(), calls=%async_computation.7 | async-start | bytes 5242880 | tf_op jit(solution)/shard_map/all_gather | solution.py:60
Sparse Core Ops, SparseCore 0:
  9.6 37.7 all-gather.2
  119.6 67.3 all-reduce.1
  189.2 34.2 all-gather.4
where the time goes:
time: 235 us; the launch traced here: 234 us
  waiting for transfers between devices  118 us (50%)
  blocking collectives  35.9 us (15%)
  other arithmetic  26.7 us (11%)
  starting transfers between devices  16.2 us (7%)
  between operations  14 us (6%)
  local copies, waits for them, and re-layouts  12.1 us (5%)
  matrix products  11.9 us (5%)
    psum x1, waiting for transfers between devices, local(): total = lax.psum(term, 'dom')  60.3 us
    all_gather x1, waiting for transfers between devices, local(): lax.all_gather(grad_projected, 'feat', axis=1, tiled=True)  34.9 us
    all_to_all x1, blocking collectives, local(): lax.all_to_all(edge_side(recv_rows), 'dom', split_axis=0, concat_axis=0,...  9.85 us
    all_to_all x1, blocking collectives, local(): lax.all_to_all(grad_message.reshape(owners, -1, cols), 'dom', split_axis=...  9.74 us
    all_to_all x1, blocking collectives, local(): lax.all_to_all(edge_side(grad_recv), 'dom', split_axis=0, concat_axis=0,...  9.74 us
    all_gather x1, waiting for transfers between devices, local(): full_rows = lax.all_gather(features, 'feat', axis=1, tiled=True)  9.58 us
    all_to_all x1, waiting for transfers between devices, local(): lax.all_to_all(message.reshape(owners, -1, cols), 'dom', split_axis=0, co...  7.34 us
    all_to_all x1, starting transfers between devices, local(): lax.all_to_all(edge.reshape(owners, -1), 'dom', split_axis=0, concat_axis...  7.28 us
  transfers between devices with their start and end apart: 6, of which 5 were waited for; matrix products, arithmetic and copies ran while one was open for 6% of the time, Pallas kernels for 0%

commit v1 on v0

--- a/solution.py
+++ b/solution.py
@@ -1,7 +1,318 @@
+import functools
+
 import jax
 import jax.numpy as jnp
 from jax import lax
+from jax.experimental import pallas as pl
+from jax.experimental.pallas import tpu as pltpu
 from jax.sharding import PartitionSpec as P
+
+MESH = pl.DeviceIdType.MESH
+LANES = 128
+VMEM_BYTES = 40 * 1024 * 1024
+
+
+def hi_lo_dot(mask, rows):
+    hi = rows.astype(jnp.bfloat16)
+    lo = (rows - hi.astype(jnp.float32)).astype(jnp.bfloat16)
+    both = jnp.concatenate([hi, lo], axis=1)
+    out = jnp.dot(mask, both, preferred_element_type=jnp.float32)
+    half = rows.shape[1]
+    return out[:, :half] + out[:, half:]
+
+
+def layer_kernel(
+    feat_ref, theta_ref, inc_ref, ew_ref, cot_ref,
+    act_ref, gf_ref, gt_ref, rep_ref,
+    meta, meta_send, meta_recv, meta_edge, v_mask, e_mask,
+    x_send, x_recv, b_send, b_recv, gx_send, gx_recv, gb_send, gb_recv,
+    theta_t, ax, gp, term, term_recv,
+    dom_send, dom_recv, feat_send, feat_recv,
+):
+    owners, cap, cols = x_send.shape
+    feats, slots, _ = ax.shape
+    nvert = feat_ref.shape[0]
+    share = gt_ref.shape[0]
+    d = lax.axis_index("dom")
+    f = lax.axis_index("feat")
+    partner = f + 1 - 2 * lax.rem(f, 2)
+    across = lax.rem(f + 2, 4)
+    diagonal = lax.rem(partner + 2, 4)
+
+    barrier = pltpu.get_barrier_semaphore()
+    for k in range(1, owners):
+        pl.semaphore_signal(
+            barrier, inc=1, device_id=(lax.rem(d + k, owners), f), device_id_type=MESH
+        )
+    for other in (partner, across, diagonal):
+        pl.semaphore_signal(barrier, inc=1, device_id=(d, other), device_id_type=MESH)
+
+    pending = []
+
+    def to_owners(phase, src, dst):
+        copies = []
+        for k in range(1, owners):
+            peer = lax.rem(d + k, owners)
+            copy = pltpu.make_async_remote_copy(
+                src_ref=src.at[peer],
+                dst_ref=dst.at[d],
+                send_sem=dom_send.at[phase, k - 1],
+                recv_sem=dom_recv.at[phase, k - 1],
+                device_id=(peer, f),
+                device_id_type=MESH,
+            )
+            copy.start()
+            copies.append(copy)
+        pending.extend(copies)
+        dst[d] = src[d]
+        return copies
+
+    def to_feat(slot, src, dst, other):
+        copy = pltpu.make_async_remote_copy(
+            src_ref=src,
+            dst_ref=dst,
+            send_sem=feat_send.at[slot],
+            recv_sem=feat_recv.at[slot],
+            device_id=(d, other),
+            device_id_type=MESH,
+        )
+        copy.start()
+        pending.append(copy)
+        return copy
+
+    def arrived(copies):
+        for copy in copies:
+            copy.wait_recv()
+
+    inc = inc_ref[...]
+    vrow = inc[0:1, :]
+    meta[...] = jnp.zeros_like(meta)
+    meta[0:1, :] = vrow.astype(jnp.float32)
+    meta[1:2, :] = inc[1:2, :].astype(jnp.float32)
+    meta[2:3, :] = inc[2:3, :].astype(jnp.float32)
+    wrow = meta[2:3, :]
+    columns = jnp.transpose(meta[...])
+    vcol = columns[:, 0:1].astype(jnp.int32)
+    wcol = columns[:, 2:3]
+    same = vcol == vrow
+    v_mask[...] = jnp.where(same, 1.0, 0.0).astype(jnp.bfloat16)
+    dvis_row = lax.rsqrt(1.0 + jnp.sum(jnp.where(same, wcol, 0.0), axis=0, keepdims=True))
+    meta[3:4, :] = wrow * dvis_row
+
+    mine = lax.rem(d, 2)
+    for o in range(owners):
+        tile = meta[:, o // 2 * LANES : (o // 2 + 1) * LANES]
+        moved = pltpu.roll(tile, cap, 1)
+        meta_send[o] = jnp.where(mine == o % 2, tile, moved)
+
+    pl.semaphore_wait(barrier, owners - 1 + feats - 1)
+    meta_copies = to_owners(0, meta_send, meta_recv)
+
+    picked = jnp.zeros((slots, 2 * cols), jnp.float32)
+    step = 512
+    lane = lax.broadcasted_iota(jnp.int32, (slots, step), 1)
+    for base in range(0, nvert, step):
+        hit = jnp.where(vcol - base == lane, 1.0, 0.0).astype(jnp.bfloat16)
+        both = jnp.concatenate(
+            [feat_ref[base : base + step, :], cot_ref[base : base + step, :]], axis=1
+        )
+        picked = picked + jnp.dot(hit, both, preferred_element_type=jnp.float32)
+    x_send[...] = picked[:, :cols].astype(jnp.bfloat16).reshape(owners, cap, cols)
+    x_copies = to_owners(1, x_send, x_recv)
+    cot = picked[:, cols:]
+
+    theta_copies = []
+    for slot, other in enumerate((partner, across, diagonal)):
+        theta_copies.append(
+            to_feat(
+                slot,
+                theta_ref.at[pl.ds(pl.multiple_of(other * cols, cols), cols), :],
+                theta_t.at[f],
+                other,
+            )
+        )
+    theta_t[f] = theta_ref[pl.ds(pl.multiple_of(f * cols, cols), cols), :]
+
+    dvis = lax.rsqrt(1.0 + jnp.sum(jnp.where(same, wrow, 0.0), axis=1, keepdims=True))
+    scale = wcol * dvis
+    sub_i = lax.broadcasted_iota(jnp.int32, (slots, slots), 0)
+    lane_i = lax.broadcasted_iota(jnp.int32, (slots, slots), 1)
+    later_row = jnp.sum(
+        jnp.where(same, jnp.where(sub_i < lane_i, 1.0, 0.0), 0.0), axis=0, keepdims=True
+    )
+    later_col = jnp.sum(
+        jnp.where(same, jnp.where(lane_i < sub_i, 1.0, 0.0), 0.0), axis=1, keepdims=True
+    )
+    rep_ref[...] = jnp.where(later_row > 0.0, -1, vrow)
+
+    arrived(meta_copies)
+    half = lax.broadcasted_iota(jnp.int32, (8, LANES), 1) < cap
+    for q in range(owners // 2):
+        meta_edge[:, q * LANES : (q + 1) * LANES] = jnp.where(
+            half, meta_recv[2 * q], meta_recv[2 * q + 1]
+        )
+    ecolumns = jnp.transpose(meta_edge[...])
+    ecol = ecolumns[:, 1:2]
+    same_edge = ecol == meta_edge[1:2, :]
+    e_mask[...] = jnp.where(same_edge, 1.0, 0.0).astype(jnp.bfloat16)
+    degree = 1.0 + jnp.sum(
+        jnp.where(same_edge, meta_edge[2:3, :], 0.0), axis=1, keepdims=True
+    )
+    sent_scale = ecolumns[:, 3:4]
+    eint = ecol.astype(jnp.int32)
+    groups = ew_ref.shape[0]
+    eweight = jnp.zeros((slots, LANES), jnp.float32)
+    for g in range(groups):
+        near = lax.broadcasted_iota(jnp.int32, (slots, LANES), 1) + g * LANES
+        eweight = jnp.where(eint == near, ew_ref[g : g + 1, :], eweight)
+    edge_scale = jnp.sum(eweight, axis=1, keepdims=True) / degree
+
+    arrived(x_copies)
+    rows = x_recv[...].reshape(slots, cols).astype(jnp.float32) * sent_scale
+    b_send[...] = (
+        (edge_scale * hi_lo_dot(e_mask[...], rows))
+        .astype(jnp.bfloat16)
+        .reshape(owners, cap, cols)
+    )
+    b_copies = to_owners(2, b_send, b_recv)
+
+    def gather_feat(slot, buf, use):
+        near = to_feat(slot, buf.at[f], buf.at[f], partner)
+        far = to_feat(slot + 1, buf.at[f], buf.at[f], across)
+        total = use(f)
+        near.wait_recv()
+        total = total + use(partner)
+        far.wait_recv()
+        relay = to_feat(slot + 2, buf.at[across], buf.at[across], partner)
+        total = total + use(across)
+        relay.wait_recv()
+        return total + use(diagonal)
+
+    arrived(b_copies)
+    back = wcol * b_recv[...].reshape(slots, cols).astype(jnp.float32)
+    ax[f] = (dvis * hi_lo_dot(v_mask[...], back)).astype(jnp.bfloat16)
+    summed = gather_feat(
+        3,
+        ax,
+        lambda j: jnp.dot(
+            ax[j],
+            theta_ref[pl.ds(pl.multiple_of(j * cols, cols), cols), :],
+            preferred_element_type=jnp.float32,
+        ),
+    )
+    sigma = jax.nn.sigmoid(summed)
+    grad = cot * (sigma * (1.0 + summed * (1.0 - sigma)))
+    gx_send[...] = (scale * grad).astype(jnp.bfloat16).reshape(owners, cap, cols)
+    gx_copies = to_owners(3, gx_send, gx_recv)
+    act_ref[...] = (summed * sigma).astype(jnp.bfloat16)
+
+    once = jnp.where(later_col > 0.0, 0.0, grad).astype(jnp.bfloat16)
+    per = cols // share
+    for j in range(feats):
+        part = lax.dot_general(
+            ax[j], once, (((0,), (0,)), ((), ())), preferred_element_type=jnp.float32
+        )
+        term[j * per : (j + 1) * per] = part.reshape(per, share, cols)
+
+    arrived(gx_copies)
+    esum = jnp.dot(
+        e_mask[...], gx_recv[...].reshape(slots, cols), preferred_element_type=jnp.float32
+    )
+    gb_send[...] = (edge_scale * esum).astype(jnp.bfloat16).reshape(owners, cap, cols)
+    gb_copies = to_owners(4, gb_send, gb_recv)
+    term_copies = to_owners(5, term, term_recv)
+
+    arrived(gb_copies)
+    gback = wcol * gb_recv[...].reshape(slots, cols).astype(jnp.float32)
+    gp[f] = (dvis * hi_lo_dot(v_mask[...], gback)).astype(jnp.bfloat16)
+    arrived(theta_copies)
+    gfeat = gather_feat(
+        6,
+        gp,
+        lambda j: lax.dot_general(
+            gp[j], theta_t[j], (((1,), (1,)), ((), ())), preferred_element_type=jnp.float32
+        ),
+    )
+    gf_ref[...] = gfeat.astype(jnp.bfloat16)
+    arrived(term_copies)
+    gt_ref[...] = jnp.sum(term_recv[...], axis=0)
+    for copy in pending:
+        copy.wait_send()
+
+
+def spread_kernel(rep_ref, act_ref, gf_ref, act_out, gf_out):
+    rows, cols = act_out.shape
+    slots = act_ref.shape[0]
+    base = pl.program_id(0) * rows
+    vertex = lax.broadcasted_iota(jnp.int32, (rows, slots), 0) + base
+    hit = jnp.where(vertex == rep_ref[...], 1.0, 0.0).astype(jnp.bfloat16)
+    both = jnp.concatenate([act_ref[...], gf_ref[...]], axis=1)
+    out = jnp.dot(hit, both, preferred_element_type=jnp.float32)
+    act_out[...] = out[:, :cols].astype(act_out.dtype)
+    gf_out[...] = out[:, cols:].astype(gf_out.dtype)
+
+
+def compact(features, theta, incidence, edge_weight, cotangent):
+    owners = lax.axis_size("dom")
+    feats = lax.axis_size("feat")
+    nvert, cols = features.shape
+    slots = incidence.shape[1]
+    cap = slots // owners
+    share = theta.shape[0] // owners
+    bf16, f32 = jnp.bfloat16, jnp.float32
+    vmem = pl.BlockSpec(memory_space=pltpu.VMEM)
+    block = pltpu.VMEM((owners, cap, cols), bf16)
+    act, gf, gt, rep = pl.pallas_call(
+        layer_kernel,
+        out_shape=(
+            jax.ShapeDtypeStruct((slots, cols), bf16),
+            jax.ShapeDtypeStruct((slots, cols), bf16),
+            jax.ShapeDtypeStruct((share, cols), f32),
+            jax.ShapeDtypeStruct((1, slots), jnp.int32),
+        ),
+        in_specs=[vmem] * 5,
+        out_specs=(vmem,) * 4,
+        scratch_shapes=[
+            pltpu.VMEM((8, slots), f32),
+            pltpu.VMEM((owners, 8, LANES), f32),
+            pltpu.VMEM((owners, 8, LANES), f32),
+            pltpu.VMEM((8, slots), f32),
+            pltpu.VMEM((slots, slots), bf16),
+            pltpu.VMEM((slots, slots), bf16),
+        ]
+        + [block] * 8
+        + [
+            pltpu.VMEM((feats, cols, cols), bf16),
+            pltpu.VMEM((feats, slots, cols), bf16),
+            pltpu.VMEM((feats, slots, cols), bf16),
+            pltpu.VMEM((owners, share, cols), f32),
+            pltpu.VMEM((owners, share, cols), f32),
+            pltpu.SemaphoreType.DMA((6, owners - 1)),
+            pltpu.SemaphoreType.DMA((6, owners - 1)),
+            pltpu.SemaphoreType.DMA((9,)),
+            pltpu.SemaphoreType.DMA((9,)),
+        ],
+        compiler_params=pltpu.CompilerParams(
+            collective_id=0, has_side_effects=True, vmem_limit_bytes=VMEM_BYTES
+        ),
+        name="layer",
+    )(features, theta, incidence, edge_weight.reshape(-1, LANES), cotangent)
+    rows = 1024
+    whole = lambda i: (0, 0)
+    activation, grad_features = pl.pallas_call(
+        spread_kernel,
+        grid=(nvert // rows,),
+        out_shape=(jax.ShapeDtypeStruct((nvert, cols), bf16),) * 2,
+        in_specs=[
+            pl.BlockSpec((1, slots), whole),
+            pl.BlockSpec((slots, cols), whole),
+            pl.BlockSpec((slots, cols), whole),
+        ],
+        out_specs=(pl.BlockSpec((rows, cols), lambda i: (i, 0)),) * 2,
+        compiler_params=pltpu.CompilerParams(vmem_limit_bytes=VMEM_BYTES),
+        name="spread",
+    )(rep, act, gf)
+    return activation, grad_features, gt
 
 
 def local(features, theta, incidence, edge_weight, cotangent):
@@ -74,8 +385,27 @@
 
 def solution(mesh):
     placed = (P("dom", "feat"), P(None, "feat"), P(None, "dom"), P("dom"), P("dom", "feat"))
+    owners, feats = mesh.shape["dom"], mesh.shape["feat"]
+
+    def program(features, theta, incidence, edge_weight, cotangent):
+        nvert, cols = features.shape
+        slots, nedge = incidence.shape[1], edge_weight.shape[0]
+        fits = (
+            feats == 4
+            and cols == LANES
+            and owners % 2 == 0
+            and slots == owners * LANES // 2
+            and slots <= 1024
+            and nvert % 1024 == 0
+            and nedge % LANES == 0
+            and theta.shape[0] % (16 * owners) == 0
+            and cols % (theta.shape[0] // owners) == 0
+        )
+        run = compact if fits else local
+        return run(features, theta, incidence, edge_weight, cotangent)
+
     return jax.shard_map(
-        local,
+        program,
         mesh=mesh,
         in_specs=placed,
         out_specs=(P("dom", "feat"), P("dom", "feat"), P("dom", "feat")),

time: 235 us -> 49 us (0.21)
  waiting for transfers between devices: 118 us -> 0 us
  Pallas kernels: 0 us -> 42.5 us
  blocking collectives: 35.9 us -> 0 us
  other arithmetic: 26.7 us -> 0 us
  starting transfers between devices: 16.2 us -> 0 us
  between operations: 14 us -> 0.65 us
  matrix products: 11.9 us -> 0 us
  local copies, waits for them, and re-layouts: 12.1 us -> 5.35 us
    psum x1 -> x0, waiting for transfers between devices: 60.3 us -> none  [local(): total = lax.psum(term, 'dom')]
    all_gather x2 -> x0, waiting for transfers between devices: 44.5 us -> none  [the longest x1 34.9 us: local(): lax.all_gather(grad_projected, 'feat', axis=1, tiled=True)]
    pallas_call x0 -> x2, Pallas kernels: none -> 42.5 us  [the longest x1 39.5 us: compact(): pl.pallas_call(layer_kernel, out_shape=(jax.ShapeDtypeStruct((slots, cols...]
    all_to_all x3 -> x0, blocking collectives: 29.3 us -> none  [the longest x1 9.85 us: local(): lax.all_to_all(edge_side(recv_rows), 'dom', split_axis=0, concat_axis=0,...]
    scatter-add x6 -> x0, other arithmetic: 18.2 us -> none  [the longest x2 6.67 us: vertex_side(): return dvis[:, None] * jax.ops.segment_sum(terms, vert, num_segments=nvert)]
    all_to_all x3 -> x0, starting transfers between devices: 16.1 us -> none  [the longest x1 7.28 us: local(): lax.all_to_all(edge.reshape(owners, -1), 'dom', split_axis=0, concat_axis...]
    dot_general x3 -> x0, matrix products: 11.9 us -> none  [the longest x1 4.41 us: local(): lax.dot_general(lax.all_gather(grad_projected, 'feat', axis=1, tiled=True...]
    all_to_all x3 -> x0, waiting for transfers between devices: 11.6 us -> none  [the longest x1 7.34 us: local(): lax.all_to_all(message.reshape(owners, -1, cols), 'dom', split_axis=0, co...]
  transfers between devices with their start and end apart: 6 -> 0, of which waited for: 5 -> 0; matrix products, arithmetic and copies ran while one was open for 6% -> 0% of each run, Pallas kernels for 0% -> 0%
where the time goes in v1:
time: 49 us; the launch traced here: 48.5 us
  Pallas kernels  42.5 us (87%)
  local copies, waits for them, and re-layouts  5.35 us (11%)
  between operations  0.65 us (1%)
    pallas_call x1, Pallas kernels, compact(): pl.pallas_call(layer_kernel, out_shape=(jax.ShapeDtypeStruct((slots, cols...  39.5 us
    unnamed x11, local copies, waits for them, and re-layouts  5.35 us
    pallas_call x1, Pallas kernels, compact(): pl.pallas_call(spread_kernel, grid=(nvert // rows,), out_shape=(jax.Shape...  2.93 us

profile of v1, /device:TPU:0, one launch (start us, length us, event | category | flops | bytes accessed | tf_op | source)
XLA Modules:
  0.0 48.5 jit_solution(16884176902623728238)
XLA Ops:
  0.6 0.0 copy-start
  0.6 1.2 %copy-done = bf16[4096,128]{1,0:T(8,128)(2,1)S(1)} copy-done((bf16[4096,128]{1,0:T(8,128)(2,1)S(1)}, bf16[4096,128]{1,0:T(8,128)(2,1)}, u32[]{:S(2)}) %copy-start) | copy-done | bytes 1048600
  1.9 0.0 copy-start.1
  1.9 1.2 %copy-done.1 = bf16[4096,128]{1,0:T(8,128)(2,1)S(1)} copy-done((bf16[4096,128]{1,0:T(8,128)(2,1)S(1)}, bf16[4096,128]{1,0:T(8,128)(2,1)}, u32[]{:S(2)}) %copy-start.1) | copy-done | bytes 1048600
  3.1 0.0 copy-start.2
  3.1 0.9 %copy-done.2 = bf16[512,128]{1,0:T(8,128)(2,1)S(1)} copy-done((bf16[512,128]{1,0:T(8,128)(2,1)S(1)}, bf16[512,128]{1,0:T(8,128)(2,1)}, u32[]{:S(2)}) %copy-start.2) | copy-done | bytes 131096
  4.0 0.0 copy-start.3
  4.0 0.7 %copy-done.3 = s32[3,512]{1,0:T(4,128)S(1)} copy-done((s32[3,512]{1,0:T(4,128)S(1)}, s32[3,512]{1,0:T(4,128)}, u32[]{:S(2)}) %copy-start.3) | copy-done | bytes 6168
  4.7 0.0 copy-start.4
  4.7 0.7 %copy-done.4 = f32[2048]{0:T(1024)S(1)} copy-done((f32[2048]{0:T(1024)S(1)}, f32[2048]{0:T(1024)}, u32[]{:S(2)}) %copy-start.4) | copy-done | bytes 8216
  5.4 39.5 %layer.1 = (bf16[512,128]{1,0:T(8,128)(2,1)S(1)}, bf16[512,128]{1,0:T(8,128)(2,1)S(1)}, f32[64,128]{1,0:T(8,128)S(1)}, s32[1,512]{1,0:T(1,128)S(1)}) custom-call(bf16[4096,128]{1,0:T(8,128)(2,1)S(1)} %copy-done, bf16[512,128]{1,0:T(8,128)(2,1)S(1)} %copy-done.2, s32[3,512]{1,0:T(4,128)S(1)} %copy-done.3, f32[16,128]{1,0:T(8,128)S(1)} %bitcast.1, ...), custom_call_target="tpu_custom_call" | custom-call | tf_op jit(solution)/shard_map/layer/pallas_call | solution.py:265
  44.9 2.9 %spread.1 = (bf16[4096,128]{1,0:T(8,128)(2,1)}, bf16[4096,128]{1,0:T(8,128)(2,1)}) custom-call(s32[1,512]{1,0:T(1,128)S(1)} %get-tuple-element.9.rep_ref, bf16[512,128]{1,0:T(8,128)(2,1)S(1)} %get-tuple-element.10.act_ref, bf16[512,128]{1,0:T(8,128)(2,1)S(1)} %get-tuple-element.11.gf_ref), custom_call_target="tpu_custom_call" | custom-call | tf_op jit(solution)/shard_map/spread/pallas_call | solution.py:302
  47.9 0.6 %copy.9 = f32[64,128]{1,0:T(8,128)} copy(f32[64,128]{1,0:T(8,128)S(1)} %get-tuple-element.20) | data formatting | bytes 65536
Async XLA Ops:
  0.6 1.2 %copy-start = (bf16[4096,128]{1,0:T(8,128)(2,1)S(1)}, bf16[4096,128]{1,0:T(8,128)(2,1)}, u32[]{:S(2)}) copy-start(bf16[4096,128]{1,0:T(8,128)(2,1)} %feat_ref.1) | copy-start | bytes 3145732
  1.9 1.2 %copy-start.1 = (bf16[4096,128]{1,0:T(8,128)(2,1)S(1)}, bf16[4096,128]{1,0:T(8,128)(2,1)}, u32[]{:S(2)}) copy-start(bf16[4096,128]{1,0:T(8,128)(2,1)} %cot_ref.1) | copy-start | bytes 3145732
  3.1 0.9 %copy-start.2 = (bf16[512,128]{1,0:T(8,128)(2,1)S(1)}, bf16[512,128]{1,0:T(8,128)(2,1)}, u32[]{:S(2)}) copy-start(bf16[512,128]{1,0:T(8,128)(2,1)} %theta_ref.1) | copy-start | bytes 393220
  4.0 0.7 %copy-start.3 = (s32[3,512]{1,0:T(4,128)S(1)}, s32[3,512]{1,0:T(4,128)}, u32[]{:S(2)}) copy-start(s32[3,512]{1,0:T(4,128)} %inc_ref.1) | copy-start | bytes 18436
  4.7 0.7 %copy-start.4 = (f32[2048]{0:T(1024)S(1)}, f32[2048]{0:T(1024)}, u32[]{:S(2)}) copy-start(f32[2048]{0:T(1024)} %param.8) | copy-start | bytes 24580

commit v2 on v1

--- a/solution.py
+++ b/solution.py
@@ -9,7 +9,7 @@
 
 MESH = pl.DeviceIdType.MESH
 LANES = 128
-VMEM_BYTES = 40 * 1024 * 1024
+VMEM_BYTES = 62 * 1024 * 1024
 
 
 def hi_lo_dot(mask, rows):
@@ -22,8 +22,9 @@
 
 
 def layer_kernel(
-    feat_ref, theta_ref, inc_ref, ew_ref, cot_ref,
+    feat_hbm, theta_hbm, inc_hbm, ew_hbm, cot_hbm,
     act_ref, gf_ref, gt_ref, rep_ref,
+    feat_ref, theta_ref, inc_ref, ew_ref, cot_ref, load_sem,
     meta, meta_send, meta_recv, meta_edge, v_mask, e_mask,
     x_send, x_recv, b_send, b_recv, gx_send, gx_recv, gb_send, gb_recv,
     theta_t, ax, gp, term, term_recv,
@@ -38,6 +39,20 @@
     partner = f + 1 - 2 * lax.rem(f, 2)
     across = lax.rem(f + 2, 4)
     diagonal = lax.rem(partner + 2, 4)
+
+    loads = []
+    for n, (src, dst) in enumerate(
+        (
+            (inc_hbm, inc_ref),
+            (feat_hbm, feat_ref),
+            (cot_hbm, cot_ref),
+            (theta_hbm, theta_ref),
+            (ew_hbm, ew_ref),
+        )
+    ):
+        load = pltpu.make_async_copy(src, dst, load_sem.at[n])
+        load.start()
+        loads.append(load)
 
     barrier = pltpu.get_barrier_semaphore()
     for k in range(1, owners):
@@ -84,6 +99,7 @@
         for copy in copies:
             copy.wait_recv()
 
+    loads[0].wait()
     inc = inc_ref[...]
     vrow = inc[0:1, :]
     meta[...] = jnp.zeros_like(meta)
@@ -105,9 +121,8 @@
         moved = pltpu.roll(tile, cap, 1)
         meta_send[o] = jnp.where(mine == o % 2, tile, moved)
 
-    pl.semaphore_wait(barrier, owners - 1 + feats - 1)
-    meta_copies = to_owners(0, meta_send, meta_recv)
-
+    loads[1].wait()
+    loads[2].wait()
     picked = jnp.zeros((slots, 2 * cols), jnp.float32)
     step = 512
     lane = lax.broadcasted_iota(jnp.int32, (slots, step), 1)
@@ -118,9 +133,12 @@
         )
         picked = picked + jnp.dot(hit, both, preferred_element_type=jnp.float32)
     x_send[...] = picked[:, :cols].astype(jnp.bfloat16).reshape(owners, cap, cols)
+    pl.semaphore_wait(barrier, owners - 1 + feats - 1)
+    meta_copies = to_owners(0, meta_send, meta_recv)
     x_copies = to_owners(1, x_send, x_recv)
     cot = picked[:, cols:]
 
+    loads[3].wait()
     theta_copies = []
     for slot, other in enumerate((partner, across, diagonal)):
         theta_copies.append(
@@ -160,6 +178,7 @@
     )
     sent_scale = ecolumns[:, 3:4]
     eint = ecol.astype(jnp.int32)
+    loads[4].wait()
     groups = ew_ref.shape[0]
     eweight = jnp.zeros((slots, LANES), jnp.float32)
     for g in range(groups):
@@ -270,9 +289,15 @@
             jax.ShapeDtypeStruct((share, cols), f32),
             jax.ShapeDtypeStruct((1, slots), jnp.int32),
         ),
-        in_specs=[vmem] * 5,
+        in_specs=[pl.BlockSpec(memory_space=pltpu.HBM)] * 5,
         out_specs=(vmem,) * 4,
         scratch_shapes=[
+            pltpu.VMEM(features.shape, bf16),
+            pltpu.VMEM(theta.shape, bf16),
+            pltpu.VMEM(incidence.shape, jnp.int32),
+            pltpu.VMEM((edge_weight.shape[0] // LANES, LANES), f32),
+            pltpu.VMEM(cotangent.shape, bf16),
+            pltpu.SemaphoreType.DMA((5,)),
             pltpu.VMEM((8, slots), f32),
             pltpu.VMEM((owners, 8, LANES), f32),
             pltpu.VMEM((owners, 8, LANES), f32),

time: 49 us -> 46.6 us (0.951)
  the two profiles are of different devices: /device:TPU:0 before, /device:TPU:15 now
where the time goes in v2:
time: 46.6 us; the launch traced here: 46.4 us
  Pallas kernels  45.1 us (97%)
  between operations  0.65 us (1%)
  local copies, waits for them, and re-layouts  0.62 us (1%)
    pallas_call x1, Pallas kernels, compact(): pl.pallas_call(layer_kernel, out_shape=(jax.ShapeDtypeStruct((slots, cols...  41.2 us
    pallas_call x1, Pallas kernels, compact(): pl.pallas_call(spread_kernel, grid=(nvert // rows,), out_shape=(jax.Shape...  3.91 us

profile of v2, /device:TPU:15, one launch (start us, length us, event | category | flops | bytes accessed | tf_op | source)
XLA Modules:
  0.0 46.4 jit_solution(1740836088693261677)
XLA Ops:
  0.6 41.2 %layer.1 = (bf16[512,128]{1,0:T(8,128)(2,1)}, bf16[512,128]{1,0:T(8,128)(2,1)}, f32[64,128]{1,0:T(8,128)}, s32[1,512]{1,0:T(1,128)}) custom-call(bf16[4096,128]{1,0:T(8,128)(2,1)} %feat_hbm.1, bf16[512,128]{1,0:T(8,128)(2,1)} %theta_hbm.1, s32[3,512]{1,0:T(4,128)} %inc_hbm.1, f32[16,128]{1,0:T(8,128)} %bitcast.1, bf16[4096,128]{1,0:T(8,128)(2,1)} %cot_hbm.1), custom_call_target="tpu_custom_call" | custom-call | tf_op jit(solution)/shard_map/layer/pallas_call | solution.py:284
  41.9 0.0 copy-start
  41.9 3.9 %spread.1 = (bf16[4096,128]{1,0:T(8,128)(2,1)}, bf16[4096,128]{1,0:T(8,128)(2,1)}) custom-call(s32[1,512]{1,0:T(1,128)} %get-tuple-element.9.rep_ref, bf16[512,128]{1,0:T(8,128)(2,1)} %get-tuple-element.10.act_ref, bf16[512,128]{1,0:T(8,128)(2,1)} %get-tuple-element.11.gf_ref), custom_call_target="tpu_custom_call" | custom-call | tf_op jit(solution)/shard_map/spread/pallas_call | solution.py:327
  45.8 0.0 copy-done
  45.8 0.6 %copy.9 = f32[64,128]{1,0:T(8,128)} copy(f32[64,128]{1,0:T(8,128)S(1)} %copy-done) | data formatting | bytes 65536
Async XLA Ops:
  41.9 3.9 %copy-start = (f32[64,128]{1,0:T(8,128)S(1)}, f32[64,128]{1,0:T(8,128)}, u32[]{:S(2)}) copy-start(f32[64,128]{1,0:T(8,128)} %get-tuple-element.20) | copy-start | bytes 98308

commit v3 on v2

--- a/solution.py
+++ b/solution.py
@@ -27,11 +27,12 @@
     feat_ref, theta_ref, inc_ref, ew_ref, cot_ref, load_sem,
     meta, meta_send, meta_recv, meta_edge, v_mask, e_mask,
     x_send, x_recv, b_send, b_recv, gx_send, gx_recv, gb_send, gb_recv,
-    theta_t, ax, gp, term, term_recv,
+    theta, cot, ax, grads, acts, term, term_recv,
     dom_send, dom_recv, feat_send, feat_recv,
 ):
     owners, cap, cols = x_send.shape
-    feats, slots, _ = ax.shape
+    slots = ax.shape[0]
+    feats = ax.shape[1] // cols
     nvert = feat_ref.shape[0]
     share = gt_ref.shape[0]
     d = lax.axis_index("dom")
@@ -82,18 +83,39 @@
         dst[d] = src[d]
         return copies
 
-    def to_feat(slot, src, dst, other):
+    def to_feat(slot, p, src, dst, other):
         copy = pltpu.make_async_remote_copy(
             src_ref=src,
             dst_ref=dst,
-            send_sem=feat_send.at[slot],
-            recv_sem=feat_recv.at[slot],
+            send_sem=feat_send.at[slot, p],
+            recv_sem=feat_recv.at[slot, p],
             device_id=(d, other),
             device_id_type=MESH,
         )
         copy.start()
         pending.append(copy)
         return copy
+
+    def block(j):
+        return pl.ds(pl.multiple_of(j * cols, cols), cols)
+
+    def part(buf, rows, j):
+        return buf.at[rows, block(j)]
+
+    def gather_start(buf, slot, pieces):
+        near, far = [], []
+        size = slots // pieces
+        for p in range(pieces):
+            rows = pl.ds(p * size, size)
+            mine_part = part(buf, rows, f)
+            far.append(to_feat(slot + 1, p, mine_part, mine_part, across))
+            near.append(to_feat(slot, p, mine_part, mine_part, partner))
+        return near, far
+
+    def relay(buf, slot, pieces, p):
+        size = slots // pieces
+        got = part(buf, pl.ds(p * size, size), across)
+        return to_feat(slot + 2, p, got, got, partner)
 
     def arrived(copies):
         for copy in copies:
@@ -121,6 +143,9 @@
         moved = pltpu.roll(tile, cap, 1)
         meta_send[o] = jnp.where(mine == o % 2, tile, moved)
 
+    pl.semaphore_wait(barrier, owners - 1 + feats - 1)
+    meta_copies = to_owners(0, meta_send, meta_recv)
+
     loads[1].wait()
     loads[2].wait()
     picked = jnp.zeros((slots, 2 * cols), jnp.float32)
@@ -133,23 +158,13 @@
         )
         picked = picked + jnp.dot(hit, both, preferred_element_type=jnp.float32)
     x_send[...] = picked[:, :cols].astype(jnp.bfloat16).reshape(owners, cap, cols)
-    pl.semaphore_wait(barrier, owners - 1 + feats - 1)
-    meta_copies = to_owners(0, meta_send, meta_recv)
     x_copies = to_owners(1, x_send, x_recv)
-    cot = picked[:, cols:]
+    cot[:, block(f)] = picked[:, cols:].astype(jnp.bfloat16)
 
     loads[3].wait()
-    theta_copies = []
-    for slot, other in enumerate((partner, across, diagonal)):
-        theta_copies.append(
-            to_feat(
-                slot,
-                theta_ref.at[pl.ds(pl.multiple_of(other * cols, cols), cols), :],
-                theta_t.at[f],
-                other,
-            )
-        )
-    theta_t[f] = theta_ref[pl.ds(pl.multiple_of(f * cols, cols), cols), :]
+    theta[:, block(f)] = theta_ref[...]
+    theta_near, theta_far = gather_start(theta, 0, feats)
+    cot_near, cot_far = gather_start(cot, 3, feats)
 
     dvis = lax.rsqrt(1.0 + jnp.sum(jnp.where(same, wrow, 0.0), axis=1, keepdims=True))
     scale = wcol * dvis
@@ -195,43 +210,65 @@
     )
     b_copies = to_owners(2, b_send, b_recv)
 
-    def gather_feat(slot, buf, use):
-        near = to_feat(slot, buf.at[f], buf.at[f], partner)
-        far = to_feat(slot + 1, buf.at[f], buf.at[f], across)
-        total = use(f)
-        near.wait_recv()
-        total = total + use(partner)
-        far.wait_recv()
-        relay = to_feat(slot + 2, buf.at[across], buf.at[across], partner)
-        total = total + use(across)
-        relay.wait_recv()
-        return total + use(diagonal)
+    theta_relay, cot_relay = [], []
+    for p in range(feats):
+        theta_far[p].wait_recv()
+        theta_relay.append(relay(theta, 0, feats, p))
+    for p in range(feats):
+        cot_far[p].wait_recv()
+        cot_relay.append(relay(cot, 3, feats, p))
 
     arrived(b_copies)
     back = wcol * b_recv[...].reshape(slots, cols).astype(jnp.float32)
-    ax[f] = (dvis * hi_lo_dot(v_mask[...], back)).astype(jnp.bfloat16)
-    summed = gather_feat(
-        3,
-        ax,
-        lambda j: jnp.dot(
-            ax[j],
-            theta_ref[pl.ds(pl.multiple_of(j * cols, cols), cols), :],
+    ax[:, block(f)] = (dvis * hi_lo_dot(v_mask[...], back)).astype(jnp.bfloat16)
+    ax_near, ax_far = gather_start(ax, 6, feats)
+    arrived(theta_near + theta_relay + cot_near + cot_relay)
+
+    gx_copies = []
+    size = slots // feats
+    per_piece = size // cap
+
+    def piece(p):
+        rows = pl.ds(p * size, size)
+        summed = jnp.dot(ax[rows, :], theta[...], preferred_element_type=jnp.float32)
+        sigma = jax.nn.sigmoid(summed)
+        slope = sigma * (1.0 + summed * (1.0 - sigma))
+        grad = (cot[rows, :].astype(jnp.float32) * slope).astype(jnp.bfloat16)
+        acts[rows, :] = (summed * sigma).astype(jnp.bfloat16)
+        grads[rows, :] = grad
+        turned = lax.dot_general(
+            grad,
+            theta[block(f), :],
+            (((1,), (1,)), ((), ())),
             preferred_element_type=jnp.float32,
-        ),
-    )
-    sigma = jax.nn.sigmoid(summed)
-    grad = cot * (sigma * (1.0 + summed * (1.0 - sigma)))
-    gx_send[...] = (scale * grad).astype(jnp.bfloat16).reshape(owners, cap, cols)
+        )
+        message = scale[p * size : (p + 1) * size] * turned
+        gx_send[p * per_piece : (p + 1) * per_piece] = message.astype(jnp.bfloat16).reshape(
+            per_piece, cap, cols
+        )
+
+    ax_relay = []
+    for p in range(feats):
+        ax_far[p].wait_recv()
+        ax_relay.append(relay(ax, 6, feats, p))
+        if p:
+            ax_near[p - 1].wait_recv()
+            ax_relay[p - 1].wait_recv()
+            piece(p - 1)
+    ax_near[feats - 1].wait_recv()
+    ax_relay[feats - 1].wait_recv()
+    piece(feats - 1)
     gx_copies = to_owners(3, gx_send, gx_recv)
-    act_ref[...] = (summed * sigma).astype(jnp.bfloat16)
-
-    once = jnp.where(later_col > 0.0, 0.0, grad).astype(jnp.bfloat16)
-    per = cols // share
-    for j in range(feats):
-        part = lax.dot_general(
-            ax[j], once, (((0,), (0,)), ((), ())), preferred_element_type=jnp.float32
-        )
-        term[j * per : (j + 1) * per] = part.reshape(per, share, cols)
+
+    once = jnp.where(later_col > 0.0, 0.0, grads[:, block(f)].astype(jnp.float32))
+    term[...] = lax.dot_general(
+        ax[...],
+        once.astype(jnp.bfloat16),
+        (((0,), (0,)), ((), ())),
+        preferred_element_type=jnp.float32,
+    ).reshape(owners, share, cols)
+    term_copies = to_owners(5, term, term_recv)
+    act_ref[...] = acts[:, block(f)]
 
     arrived(gx_copies)
     esum = jnp.dot(
@@ -239,27 +276,17 @@
     )
     gb_send[...] = (edge_scale * esum).astype(jnp.bfloat16).reshape(owners, cap, cols)
     gb_copies = to_owners(4, gb_send, gb_recv)
-    term_copies = to_owners(5, term, term_recv)
 
     arrived(gb_copies)
     gback = wcol * gb_recv[...].reshape(slots, cols).astype(jnp.float32)
-    gp[f] = (dvis * hi_lo_dot(v_mask[...], gback)).astype(jnp.bfloat16)
-    arrived(theta_copies)
-    gfeat = gather_feat(
-        6,
-        gp,
-        lambda j: lax.dot_general(
-            gp[j], theta_t[j], (((1,), (1,)), ((), ())), preferred_element_type=jnp.float32
-        ),
-    )
-    gf_ref[...] = gfeat.astype(jnp.bfloat16)
+    gf_ref[...] = (dvis * hi_lo_dot(v_mask[...], gback)).astype(jnp.bfloat16)
     arrived(term_copies)
     gt_ref[...] = jnp.sum(term_recv[...], axis=0)
     for copy in pending:
         copy.wait_send()
 
 
-def spread_kernel(rep_ref, act_ref, gf_ref, act_out, gf_out):
+def spread_kernel(rep_ref, act_ref, gf_ref, gt_ref, act_out, gf_out, gt_out):
     rows, cols = act_out.shape
     slots = act_ref.shape[0]
     base = pl.program_id(0) * rows
@@ -269,6 +296,7 @@
     out = jnp.dot(hit, both, preferred_element_type=jnp.float32)
     act_out[...] = out[:, :cols].astype(act_out.dtype)
     gf_out[...] = out[:, cols:].astype(gf_out.dtype)
+    gt_out[...] = gt_ref[...]
 
 
 def compact(features, theta, incidence, edge_weight, cotangent):
@@ -278,6 +306,7 @@
     slots = incidence.shape[1]
     cap = slots // owners
     share = theta.shape[0] // owners
+    whole_theta = (theta.shape[0], feats * cols)
     bf16, f32 = jnp.bfloat16, jnp.float32
     vmem = pl.BlockSpec(memory_space=pltpu.VMEM)
     block = pltpu.VMEM((owners, cap, cols), bf16)
@@ -307,15 +336,17 @@
         ]
         + [block] * 8
         + [
-            pltpu.VMEM((feats, cols, cols), bf16),
-            pltpu.VMEM((feats, slots, cols), bf16),
-            pltpu.VMEM((feats, slots, cols), bf16),
+            pltpu.VMEM(whole_theta, bf16),
+            pltpu.VMEM((slots, feats * cols), bf16),
+            pltpu.VMEM((slots, feats * cols), bf16),
+            pltpu.VMEM((slots, feats * cols), bf16),
+            pltpu.VMEM((slots, feats * cols), bf16),
             pltpu.VMEM((owners, share, cols), f32),
             pltpu.VMEM((owners, share, cols), f32),
             pltpu.SemaphoreType.DMA((6, owners - 1)),
             pltpu.SemaphoreType.DMA((6, owners - 1)),
-            pltpu.SemaphoreType.DMA((9,)),
-            pltpu.SemaphoreType.DMA((9,)),
+            pltpu.SemaphoreType.DMA((9, feats)),
+            pltpu.SemaphoreType.DMA((9, feats)),
         ],
         compiler_params=pltpu.CompilerParams(
             collective_id=0, has_side_effects=True, vmem_limit_bytes=VMEM_BYTES
@@ -324,20 +355,23 @@
     )(features, theta, incidence, edge_weight.reshape(-1, LANES), cotangent)
     rows = 1024
     whole = lambda i: (0, 0)
-    activation, grad_features = pl.pallas_call(
+    activation, grad_features, grad_theta = pl.pallas_call(
         spread_kernel,
         grid=(nvert // rows,),
-        out_shape=(jax.ShapeDtypeStruct((nvert, cols), bf16),) * 2,
+        out_shape=(jax.ShapeDtypeStruct((nvert, cols), bf16),) * 2
+        + (jax.ShapeDtypeStruct((share, cols), f32),),
         in_specs=[
             pl.BlockSpec((1, slots), whole),
             pl.BlockSpec((slots, cols), whole),
             pl.BlockSpec((slots, cols), whole),
+            pl.BlockSpec((share, cols), whole),
         ],
-        out_specs=(pl.BlockSpec((rows, cols), lambda i: (i, 0)),) * 2,
+        out_specs=(pl.BlockSpec((rows, cols), lambda i: (i, 0)),) * 2
+        + (pl.BlockSpec((share, cols), whole),),
         compiler_params=pltpu.CompilerParams(vmem_limit_bytes=VMEM_BYTES),
         name="spread",
-    )(rep, act, gf)
-    return activation, grad_features, gt
+    )(rep, act, gf, gt)
+    return activation, grad_features, grad_theta
 
 
 def local(features, theta, incidence, edge_weight, cotangent):
@@ -420,7 +454,7 @@
             and cols == LANES
             and owners % 2 == 0
             and slots == owners * LANES // 2
-            and slots <= 1024
+            and slots == theta.shape[0] == feats * cols
             and nvert % 1024 == 0
             and nedge % LANES == 0
             and theta.shape[0] % (16 * owners) == 0

time: 46.6 us -> 45.1 us (0.968)
  the two profiles are of different devices: /device:TPU:15 before, /device:TPU:0 now
where the time goes in v3:
time: 45.1 us; the launch traced here: 44.9 us
  Pallas kernels  44.3 us (98%)
  between operations  0.64 us (1%)
    pallas_call x1, Pallas kernels, compact(): pl.pallas_call(layer_kernel, out_shape=(jax.ShapeDtypeStruct((slots, cols...  40.4 us
    pallas_call x1, Pallas kernels, compact(): pl.pallas_call(spread_kernel, grid=(nvert // rows,), out_shape=(jax.Shape...  3.93 us

profile of v3, /device:TPU:0, one launch (start us, length us, event | category | flops | bytes accessed | tf_op | source)
XLA Modules:
  0.0 44.9 jit_solution(5153133473878488073)
XLA Ops:
  0.6 40.4 %layer.1 = (bf16[512,128]{1,0:T(8,128)(2,1)}, bf16[512,128]{1,0:T(8,128)(2,1)}, f32[64,128]{1,0:T(8,128)}, s32[1,512]{1,0:T(1,128)}) custom-call(bf16[4096,128]{1,0:T(8,128)(2,1)} %feat_hbm.1, bf16[512,128]{1,0:T(8,128)(2,1)} %theta_hbm.1, s32[3,512]{1,0:T(4,128)} %inc_hbm.1, f32[16,128]{1,0:T(8,128)} %bitcast.1, bf16[4096,128]{1,0:T(8,128)(2,1)} %cot_hbm.1), custom_call_target="tpu_custom_call" | custom-call | tf_op jit(solution)/shard_map/layer/pallas_call | solution.py:313
  41.0 3.9 %spread.1 = (bf16[4096,128]{1,0:T(8,128)(2,1)}, bf16[4096,128]{1,0:T(8,128)(2,1)}, f32[64,128]{1,0:T(8,128)}) custom-call(s32[1,512]{1,0:T(1,128)} %get-tuple-element.7.rep_ref, bf16[512,128]{1,0:T(8,128)(2,1)} %get-tuple-element.8.act_ref, bf16[512,128]{1,0:T(8,128)(2,1)} %get-tuple-element.9.gf_ref, f32[64,128]{1,0:T(8,128)} %get-tuple-element.10.gt_ref), custom_call_target="tpu_custom_call" | custom-call | tf_op jit(solution)/shard_map/spread/pallas_call | solution.py:358

commit v4 on v3

--- a/solution.py
+++ b/solution.py
@@ -266,8 +266,7 @@
         once.astype(jnp.bfloat16),
         (((0,), (0,)), ((), ())),
         preferred_element_type=jnp.float32,
-    ).reshape(owners, share, cols)
-    term_copies = to_owners(5, term, term_recv)
+    ).astype(jnp.bfloat16).reshape(owners, share, cols)
     act_ref[...] = acts[:, block(f)]
 
     arrived(gx_copies)
@@ -276,12 +275,13 @@
     )
     gb_send[...] = (edge_scale * esum).astype(jnp.bfloat16).reshape(owners, cap, cols)
     gb_copies = to_owners(4, gb_send, gb_recv)
+    term_copies = to_owners(5, term, term_recv)
 
     arrived(gb_copies)
     gback = wcol * gb_recv[...].reshape(slots, cols).astype(jnp.float32)
     gf_ref[...] = (dvis * hi_lo_dot(v_mask[...], gback)).astype(jnp.bfloat16)
     arrived(term_copies)
-    gt_ref[...] = jnp.sum(term_recv[...], axis=0)
+    gt_ref[...] = jnp.sum(term_recv[...].astype(jnp.float32), axis=0)
     for copy in pending:
         copy.wait_send()
 
@@ -341,8 +341,8 @@
             pltpu.VMEM((slots, feats * cols), bf16),
             pltpu.VMEM((slots, feats * cols), bf16),
             pltpu.VMEM((slots, feats * cols), bf16),
-            pltpu.VMEM((owners, share, cols), f32),
-            pltpu.VMEM((owners, share, cols), f32),
+            pltpu.VMEM((owners, share, cols), bf16),
+            pltpu.VMEM((owners, share, cols), bf16),
             pltpu.SemaphoreType.DMA((6, owners - 1)),
             pltpu.SemaphoreType.DMA((6, owners - 1)),
             pltpu.SemaphoreType.DMA((9, feats)),
@@ -353,7 +353,7 @@
         ),
         name="layer",
     )(features, theta, incidence, edge_weight.reshape(-1, LANES), cotangent)
-    rows = 1024
+    rows = 2048
     whole = lambda i: (0, 0)
     activation, grad_features, grad_theta = pl.pallas_call(
         spread_kernel,

time: 45.1 us -> 42.6 us (0.945)
  Pallas kernels: 44.3 us -> 41.8 us
    pallas_call x1, Pallas kernels: 40.4 us -> 38.4 us  [compact(): pl.pallas_call(layer_kernel, out_shape=(jax.ShapeDtypeStruct((slots, cols...]
    pallas_call x1, Pallas kernels: 3.93 us -> 3.43 us  [compact(): pl.pallas_call(spread_kernel, grid=(nvert // rows,), out_shape=(jax.Shape...]
where the time goes in v4:
time: 42.6 us; the launch traced here: 42.4 us
  Pallas kernels  41.8 us (98%)
  between operations  0.64 us (2%)
    pallas_call x1, Pallas kernels, compact(): pl.pallas_call(layer_kernel, out_shape=(jax.ShapeDtypeStruct((slots, cols...  38.4 us
    pallas_call x1, Pallas kernels, compact(): pl.pallas_call(spread_kernel, grid=(nvert // rows,), out_shape=(jax.Shape...  3.43 us

profile of v4, /device:TPU:0, one launch (start us, length us, event | category | flops | bytes accessed | tf_op | source)
XLA Modules:
  0.0 42.4 jit_solution(3564951611740861868)
XLA Ops:
  0.6 38.4 %layer.1 = (bf16[512,128]{1,0:T(8,128)(2,1)}, bf16[512,128]{1,0:T(8,128)(2,1)}, f32[64,128]{1,0:T(8,128)}, s32[1,512]{1,0:T(1,128)}) custom-call(bf16[4096,128]{1,0:T(8,128)(2,1)} %feat_hbm.1, bf16[512,128]{1,0:T(8,128)(2,1)} %theta_hbm.1, s32[3,512]{1,0:T(4,128)} %inc_hbm.1, f32[16,128]{1,0:T(8,128)} %bitcast.1, bf16[4096,128]{1,0:T(8,128)(2,1)} %cot_hbm.1), custom_call_target="tpu_custom_call" | custom-call | tf_op jit(solution)/shard_map/layer/pallas_call | solution.py:313
  39.0 3.4 %spread.1 = (bf16[4096,128]{1,0:T(8,128)(2,1)}, bf16[4096,128]{1,0:T(8,128)(2,1)}, f32[64,128]{1,0:T(8,128)}) custom-call(s32[1,512]{1,0:T(1,128)} %get-tuple-element.7.rep_ref, bf16[512,128]{1,0:T(8,128)(2,1)} %get-tuple-element.8.act_ref, bf16[512,128]{1,0:T(8,128)(2,1)} %get-tuple-element.9.gf_ref, f32[64,128]{1,0:T(8,128)} %get-tuple-element.10.gt_ref), custom_call_target="tpu_custom_call" | custom-call | tf_op jit(solution)/shard_map/spread/pallas_call | solution.py:358
